TPU v7x, 32 devices: a whole 2x2x4 slice. The times are simulated.
32 devices in a mesh: groups: 2 (over y), space: 4 (over z), date: 2 (over x), band: 2 (over core).
Axes of the slice: x: 2, y: 2, z: 4, core: 2. Of those that a mesh axis runs over, the one named last changes fastest.
Arguments:
- reflect: float32 [16, 8, 256, 256], P('date', 'band', ('groups', 'space')), parts along dimension 2, may hold values from -6 to 6
- kernels: float32 [3, 8, 33], P(None, 'band'), may hold values from 0.2 to 2
- strength: float32 [3, 8], P(None, 'band'), may hold values from 0.2 to 0.6
- destinations: int32 [128, 1], P(('groups', 'space')), parts along dimension 0, may hold values from 0 to 3; in each aligned block of 16 rows (0 to 15, 16 to 31, ...) at most 8 rows name the same one
- offsets: int32 [128], P(('groups', 'space')), parts along dimension 0, may hold values from 0 to 60
- counts: int32 [16, 8], P('date', ('groups', 'space')), parts along dimension 1, may hold values from 1 to 8192
- resample_rows: float32 [8, 4, 4], P(('groups', 'space')), parts along dimension 0, may hold values from -3 to 3
- resample_columns: float32 [8, 128, 128], P(('groups', 'space')), parts along dimension 0, may hold values from -0.5 to 0.5
Outputs:
- geomedian: float32 [8, 512, 128], P('band', ('groups', 'space')), parts along dimension 1
There are 2 independent parts, one for each index of `groups`. A program takes and returns all parts, laid end to end along the dimension named above; an argument that names none is the same for every part. Nothing has to cross between parts.
Inputs may be any that keep to these rules, and one draw needn't show every extreme that they name: `destinations`: in each aligned block of 16 entries (the blocks of one strip) no tile is named more than 8 times, a bound that some block reaches.
All inputs are finite; a program needn't handle non-finite values.
Results may differ from a plain program's by a relative error of at most 0.00011.
Values sent between devices are 32-bit elements; how exact they have to be, the bound alone decides.
A program may use at most 128 MiB of HBM per device.

v0:
```python
import jax
import jax.numpy as jnp
from jax import lax
from jax.sharding import PartitionSpec as P

BROWS = 4
BCOLS = 128
ITERS = 4


highest = lax.Precision.HIGHEST
smooth_sq = 0.01


def padded_2(block, sides, width):
    for axis, dim in sides:
        count = lax.axis_size(axis)
        forward = [(i, i + 1) for i in range(count - 1)]
        backward = [(target, source) for source, target in forward]
        low = lax.ppermute(
            lax.slice_in_dim(block, block.shape[dim] - width, None, axis=dim), axis, forward
        )
        high = lax.ppermute(lax.slice_in_dim(block, 0, width, axis=dim), axis, backward)
        block = jnp.concatenate([low, block, high], axis=dim)
    return block


def band_matrix(weights, count_out, count_in, lead_shift):
    tap_count = weights.shape[1]
    offset = jnp.arange(count_in)[None, :] - jnp.arange(count_out)[:, None] + lead_shift
    matrix = jnp.zeros((weights.shape[0], count_out, count_in), jnp.float32)
    for tap_index in range(tap_count):
        chosen = (offset == tap_index).astype(jnp.float32)
        matrix = matrix + weights[:, tap_index, None, None] * chosen[None, :, :]
    return matrix


def correct_strip(values, kernels, strength):
    radius = (kernels.shape[2] - 1) // 2
    strip_rows = values.shape[2]
    column_count = values.shape[3]
    for pass_index in range(kernels.shape[0]):
        norm_taps = kernels[pass_index] / jnp.sum(kernels[pass_index], axis=1, keepdims=True)
        row_matrix = band_matrix(norm_taps, strip_rows, strip_rows + 2 * radius, 0)
        column_matrix = band_matrix(norm_taps, column_count, column_count, radius)
        padded = padded_2(values, (("space", 2),), radius)
        row_pass = jnp.einsum("bij,tbjc->tbic", row_matrix, padded, precision=highest)
        blurred = jnp.einsum("tbrj,bcj->tbrc", row_pass, column_matrix, precision=highest)
        values = values + strength[pass_index][None, :, None, None] * (values - blurred)
    return values


def cut_blocks(values):
    date_here, band_here, strip_rows, column_count = values.shape
    shaped = values.reshape(
        date_here, band_here, strip_rows // BROWS, BROWS, column_count // BCOLS, BCOLS
    )
    return shaped.transpose(2, 4, 0, 1, 3, 5).reshape(-1, date_here, band_here, BROWS, BCOLS)


def pack_slots(blocks, targets, starts, tile_count, capacity):
    onehot = (targets[:, None] == jnp.arange(tile_count)[None, :]).astype(jnp.int32)
    before = jnp.cumsum(onehot, axis=0) - onehot
    ranked = jnp.sum(before * onehot, axis=1)
    slot_index = targets * capacity + ranked
    placer = (slot_index[None, :] == jnp.arange(tile_count * capacity)[:, None]).astype(jnp.float32)
    packed = jnp.einsum("sn,ntbrc->stbrc", placer, blocks, precision=highest)
    moved_starts = jnp.dot(placer, starts.astype(jnp.float32), precision=highest)
    shape_out = (tile_count, capacity) + blocks.shape[1:]
    return (packed.reshape(shape_out), moved_starts.reshape(tile_count, capacity))


def lay_tile(slot_data, slot_starts, tile_rows):
    flat_rows = slot_data.reshape((-1,) + slot_data.shape[2:])
    first_row = slot_starts.reshape(-1).astype(jnp.int32)
    target_row = first_row[:, None] + jnp.arange(BROWS, dtype=jnp.int32)[None, :]
    placer = (
        target_row[:, :, None] == jnp.arange(tile_rows, dtype=jnp.int32)[None, None, :]
    ).astype(jnp.float32)
    return jnp.einsum("sij,stbic->tbjc", placer, flat_rows, precision=highest)


def band_total(squares):
    return lax.psum(squares, "band")


def keep_local(numerator, denominator):
    return (numerator, denominator)


def geomedian_steps(stacked, weight_column, combine):
    numerator = jnp.sum(weight_column[:, :, None] * stacked, axis=0)
    denominator = jnp.sum(weight_column) * jnp.ones((stacked.shape[2],), jnp.float32)
    numerator, denominator = combine(numerator, denominator)
    estimate = numerator / denominator[None, :]
    for iter_index in range(ITERS):
        partial_sq = jnp.sum((stacked - estimate[None]) ** 2, axis=1)
        distance = jnp.sqrt(band_total(partial_sq) + smooth_sq)
        scaled = weight_column / distance
        numerator = jnp.sum(scaled[:, None, :] * stacked, axis=0)
        denominator = jnp.sum(scaled, axis=0)
        numerator, denominator = combine(numerator, denominator)
        estimate = numerator / denominator[None, :]
    return estimate


def local(
    reflect, kernels, strength, destinations, offsets, counts, resample_rows, resample_columns
):
    corrected = correct_strip(reflect, kernels, strength)
    blocks = cut_blocks(corrected)
    tile_count = lax.axis_size("space")
    block_count = blocks.shape[0]
    capacity = max(2, 2 * block_count // tile_count)
    targets = destinations[:, 0]
    count_here = counts.astype(jnp.float32)
    count_part = jnp.sum(count_here)
    packed, starts = pack_slots(blocks, targets, offsets, tile_count, capacity)
    own_rows = resample_rows[0]
    own_columns = resample_columns[0]
    raw_blocks = lax.all_to_all(packed, "space", split_axis=0, concat_axis=0, tiled=True)
    raw_starts = lax.all_to_all(starts, "space", split_axis=0, concat_axis=0, tiled=True)
    row_pass = jnp.einsum("ij,smtbjc->smtbic", own_rows, raw_blocks, precision=highest)
    final_blocks = jnp.einsum("smtbic,cv->smtbiv", row_pass, own_columns, precision=highest)
    tile_rows = block_count * BROWS
    assembled = lay_tile(final_blocks, raw_starts, tile_rows)
    count_sum = lax.psum(count_part, ("space", "date"))
    mean_count = count_sum / (counts.shape[0] * lax.axis_size("date") * tile_count)
    weight_column = count_here / (count_here + mean_count)
    date_here = assembled.shape[0]
    band_here = assembled.shape[1]
    pixels = tile_rows * BCOLS
    stacked = assembled.reshape(date_here, band_here, pixels)
    date_count = lax.axis_size("date")
    spread = jnp.broadcast_to(weight_column[:, :, None], (date_here, 1, date_count))
    whole_stack, whole_weight = (
        lax.all_to_all(stacked, "date", split_axis=2, concat_axis=0, tiled=True),
        lax.all_to_all(spread, "date", split_axis=2, concat_axis=0, tiled=True),
    )
    part_estimate = geomedian_steps(whole_stack, whole_weight.reshape(-1, 1), keep_local)
    estimate = lax.all_gather(part_estimate, "date", axis=1, tiled=True)
    return estimate.reshape(band_here, tile_rows, BCOLS)


def solution(mesh):
    in_specs = (
        P("date", "band", ("groups", "space"), None),
        P(None, "band", None),
        P(None, "band"),
        P(("groups", "space"), None),
        P(("groups", "space")),
        P("date", ("groups", "space")),
        P(("groups", "space"), None, None),
        P(("groups", "space"), None, None),
    )
    out_specs = P("band", ("groups", "space"), None)
    return jax.shard_map(local, mesh=mesh, in_specs=in_specs, out_specs=out_specs, check_vma=False)
```

profile of v0, /device:TPU:0, one launch (start us, length us, event | category | flops | bytes accessed | tf_op | source)
XLA Modules:
  0.0 362.3 jit_solution(205824982258235343)
XLA Ops:
  6.5 1.3 fusion.1005
  7.9 5.0 %collective-permute-start = (f32[8,4,16,256]{3,2,0,1:T(8,128)S(1)}, f32[8,4,16,256]{3,2,0,1:T(8,128)S(1)}, u32[]{:S(2)}, u32[]{:S(2)}) collective-permute-start(f32[8,4,16,256]{3,2,0,1:T(8,128)S(1)} %get-tuple-element.111), channel_id=1, source_target_pairs={{0,4},{4,8},{8,12},{1,5},{5,9},{9,13},{2,6},{6,10},{10,14},{3,7},{... | collective-permute-start | bytes 1572872 | tf_op jit(solution)/shard_map/ppermute | solution.py:20
  12.9 1.3 collective-permute-start.1
  15.4 0.6 fusion.969
  16.0 0.6 fusion.971
  17.3 0.6 fusion.975
  20.9 0.6 fusion.987
  21.5 0.6 fusion.989
  23.1 0.6 fusion.991
  24.4 3.7 %collective-permute-done.1 = f32[8,4,16,256]{3,2,0,1:T(8,128)S(1)} collective-permute-done((f32[8,4,16,256]{3,2,0,1:T(8,128)S(1)}, f32[8,4,16,256]{3,2,0,1:T(8,128)S(1)}, u32[]{:S(2)}, u32[]{:S(2)}) %collective-permute-start.1) | collective-permute-done | bytes 524320 | tf_op jit(solution)/shard_map/ppermute | solution.py:23
  28.2 2.6 fusion.28
  31.1 4.4 %fusion.39 = f32[8,4,32,256]{3,2,0,1:T(8,128)S(1)} fusion(f32[8,4,32,256]{3,2,0,1:T(8,128)S(1)} %fusion.28, f32[256,256]{1,0:T(8,128)S(1)} %fusion.517, f32[4]{0:T(128)S(1)} %get-tuple-element.75, f32[256,256]{1,0:T(8,128)S(1)} %get-tuple-element.190, f32[4]{0:T(128)S(1)} %get-tuple-element.76, f32[256,256]{1,0:T(8,128)S(1)} %get-tuple-element.189, ...), kind=kOutput, calls=%fused_computation.37 | convolution fusion | flops 823132160 | bytes 11797024 | tf_op jit(solution)/shard_map/tbrj,bcj->tbrc/dot_general | solution.py:48
  35.6 4.3 %collective-permute-start.2 = (f32[8,4,16,256]{3,2,0,1:T(8,128)S(1)}, f32[8,4,16,256]{3,2,0,1:T(8,128)}, u32[]{:S(2)}, u32[]{:S(2)}) collective-permute-start(f32[8,4,16,256]{3,2,0,1:T(8,128)S(1)} %get-tuple-element.109), channel_id=1, source_target_pairs={{0,4},{4,8},{8,12},{1,5},{5,9},{9,13},{2,6},{6,10},{10,14},{3,7},{... | collective-permute-start | bytes 1572872 | tf_op jit(solution)/shard_map/ppermute | solution.py:20
  39.8 1.5 collective-permute-start.3
  42.7 6.3 %collective-permute-done.2 = f32[8,4,16,256]{3,2,0,1:T(8,128)} collective-permute-done((f32[8,4,16,256]{3,2,0,1:T(8,128)S(1)}, f32[8,4,16,256]{3,2,0,1:T(8,128)}, u32[]{:S(2)}, u32[]{:S(2)}) %collective-permute-start.2) | collective-permute-done | bytes 524320 | tf_op jit(solution)/shard_map/ppermute | solution.py:20
  49.0 5.0 %collective-permute-done.3 = f32[8,4,16,256]{3,2,0,1:T(8,128)} collective-permute-done((f32[8,4,16,256]{3,2,0,1:T(8,128)S(1)}, f32[8,4,16,256]{3,2,0,1:T(8,128)}, u32[]{:S(2)}, u32[]{:S(2)}) %collective-permute-start.3) | collective-permute-done | bytes 524320 | tf_op jit(solution)/shard_map/ppermute | solution.py:23
  54.0 2.8 fusion.25
  57.0 6.2 %fusion.36 = f32[8,4,32,256]{3,2,0,1:T(8,128)S(1)} fusion(f32[8,4,32,256]{3,2,0,1:T(8,128)S(1)} %fusion.39, f32[8,4,32,256]{3,2,0,1:T(8,128)S(1)} %fusion.25, f32[4]{0:T(128)S(1)} %get-tuple-element.42, f32[4]{0:T(128)S(1)} %get-tuple-element.43, f32[4]{0:T(128)S(1)} %get-tuple-element.44, f32[4]{0:T(128)S(1)} %get-tuple-element.45, ...), kind=kOutput, calls=%fused_computation.33 | convolution fusion | flops 823132160 | bytes 11797024 | tf_op jit(solution)/shard_map/tbrj,bcj->tbrc/dot_general | solution.py:48
  63.4 2.7 collective-permute-start.4
  66.2 1.3 collective-permute-start.5
  67.6 0.7 all_to_all.35
  68.3 4.2 %all-to-all-start.2 = ((f32[4,1,8]{2,1,0:T(1,128)}), f32[4,1,8]{2,1,0:T(1,128)S(1)}, u32[]{:S(2)}, u32[]{:S(2)}) async-start(f32[4,1,8]{2,1,0:T(1,128)} %bitcast.43), calls=%async_computation.2 | async-start | bytes 4096 | tf_op jit(solution)/shard_map/all_to_all | solution.py:122
  73.4 1.6 collective-permute-done.4
  74.9 4.3 %collective-permute-done.5 = f32[8,4,16,256]{3,2,0,1:T(8,128)} collective-permute-done((f32[8,4,16,256]{3,2,0,1:T(8,128)S(1)}, f32[8,4,16,256]{3,2,0,1:T(8,128)}, u32[]{:S(2)}, u32[]{:S(2)}) %collective-permute-start.5) | collective-permute-done | bytes 524320 | tf_op jit(solution)/shard_map/ppermute | solution.py:23
  79.2 2.7 fusion.22
  82.0 7.3 %fusion.33 = f32[8,4,32,256]{3,2,0,1:T(8,128)S(1)} fusion(f32[8,4,32,256]{3,2,0,1:T(8,128)S(1)} %fusion.36, f32[8,4,32,256]{3,2,0,1:T(8,128)S(1)} %fusion.22, f32[4]{0:T(128)S(1)} %get-tuple-element.9, f32[4]{0:T(128)S(1)} %get-tuple-element.10, f32[4]{0:T(128)S(1)} %get-tuple-element.11, f32[4]{0:T(128)S(1)} %get-tuple-element.12, ...), kind=kOutput, calls=%fused_computation.29 | convolution fusion | flops 823132160 | bytes 11797024 | tf_op jit(solution)/shard_map/tbrj,bcj->tbrc/dot_general | solution.py:48
  89.9 0.6 copy.63
  90.5 2.8 fusion.56
  93.3 3.7 %all-to-all-start.1 = ((f32[4,8,8,4,4,128]{5,1,4,3,2,0:T(8,128)}), f32[4,8,8,4,4,128]{5,1,4,3,2,0:T(8,128)S(1)}, u32[]{:S(2)}, u32[]{:S(2)}) async-start(f32[4,8,8,4,4,128]{5,1,4,3,2,0:T(8,128)} %fusion.56), calls=%async_computation.1 | async-start | bytes 4194304 | tf_op jit(solution)/shard_map/all_to_all | solution.py:121
  97.7 45.5 %psum.35 = f32[]{:T(128)} all-reduce(f32[]{:T(128)} %convert_reduce_fusion.1), channel_id=1, replica_groups=mesh['groups'=2,'space'=4,'date'=2,'band'=2] {'space','date'}, use_global_device_ids=true, to_apply=%region_1.0 | all-reduce | flops 1 | bytes 8 | tf_op jit(solution)/shard_map/psum | solution.py:127
  144.5 9.1 %all-to-all-start = ((f32[8,1,2]{0,1,2:T(1,128)}), f32[8,1,2]{0,1,2:T(1,128)S(1)}, u32[]{:S(2)}, u32[]{:S(2)}) async-start(f32[8,1,2]{0,1,2:T(1,128)} %broadcast_in_dim.5), calls=%async_computation | async-start | bytes 2048 | tf_op jit(solution)/shard_map/all_to_all | solution.py:138
  153.6 3.8 %fusion.20 = f32[4,8,8,4,128,4]{4,5,3,2,1,0:T(4,128)S(1)} fusion(f32[4,8,8,4,4,128]{5,1,4,3,2,0:T(8,128)S(1)} %all-to-all-done.1, f32[1,4,4]{2,1,0:T(4,128)S(1)} %copy-done.65), kind=kOutput, calls=%fused_computation.20 | convolution fusion | flops 25165824 | bytes 4194368 | tf_op jit(solution)/shard_map/ij,smtbjc->smtbic/dot_general | solution.py:123
  157.5 3.1 fusion.18
  160.6 1.0 convolution_bitcast_fusion
  161.6 8.6 %copy.90 = f32[8,4,64,128]{0,1,3,2:T(4,128)} copy(f32[8,4,64,128]{3,2,1,0:T(8,128)S(1)} %convolution_bitcast_fusion) | data formatting | bytes 2097152 | tf_op jit(solution)/shard_map/reshape | solution.py:133
  170.2 28.1 %reshape.1121 = f32[2,1,131072]{2,1,0:T(1,128)} reshape(f32[8192,4,8]{2,1,0:T(4,128)} %bitcast.199) | data formatting | bytes 2097152
  198.3 3.6 all-to-all-start.3
  202.8 9.7 %all-to-all-done.3 = f32[2,1,131072]{2,1,0:T(1,128)S(1)} async-done(((f32[2,1,131072]{2,1,0:T(1,128)}), f32[2,1,131072]{2,1,0:T(1,128)S(1)}, u32[]{:S(2)}, u32[]{:S(2)}) %all-to-all-start.3) | async-done | bytes 1048608 | tf_op jit(solution)/shard_map/all_to_all | solution.py:137
  213.0 4.0 %reduce.217 = f32[2,131072]{1,0:T(2,128)S(1)} reduce(f32[2,1,131072]{2,1,0:T(1,128)S(1)} %all-to-all-done.3, f32[]{:T(128)} %broadcast.1279), dimensions={1}, to_apply=%all_to_all.37.reduce_sub_computation | reduce | bytes 2097156 | tf_op jit(solution)/shard_map/all_to_all | solution.py:137
  217.0 26.1 %reshape.1122 = f32[8192,4,8]{2,1,0:T(4,128)} reshape(f32[2,131072]{1,0:T(2,128)S(1)} %reduce.217) | data formatting | bytes 2097152
  243.1 13.2 %copy.69 = f32[8,4,2,4096]{3,2,1,0:T(2,128)S(1)} copy(f32[8,4,2,4096]{0,1,3,2:T(4,128)} %bitcast.200) | data formatting | bytes 2097152 | tf_op jit(solution)/shard_map/all_to_all | solution.py:137
  256.3 0.7 fusion.43
  257.5 0.7 fusion.45
  258.2 0.9 copy.114
  259.2 19.2 %all-reduce.5.cloned.1.call-done = f32[16,4096]{1,0:T(8,128)} async-done(((f32[16,4096]{1,0:T(8,128)}), f32[16,4096]{1,0:T(8,128)}) %all-reduce.5.cloned.1.call-update) | async-done | bytes 262160 | tf_op jit(solution)/shard_map/psum | solution.py:84
  278.4 1.1 fusion.518
  279.6 0.7 fusion.46
  280.3 0.7 fusion.48
  281.0 0.9 copy.113
  281.9 19.5 %all-reduce.7.cloned.1.call-done = f32[16,4096]{1,0:T(8,128)} async-done(((f32[16,4096]{1,0:T(8,128)}), f32[16,4096]{1,0:T(8,128)}) %all-reduce.7.cloned.1.call-update) | async-done | bytes 262160 | tf_op jit(solution)/shard_map/psum | solution.py:84
  301.5 1.1 fusion.520
  302.8 0.7 fusion.49
  303.5 0.7 fusion.51
  304.1 0.9 copy.112
  305.3 19.2 %all-reduce.9.cloned.1.call-done = f32[16,4096]{1,0:T(8,128)} async-done(((f32[16,4096]{1,0:T(8,128)}), f32[16,4096]{1,0:T(8,128)}) %all-reduce.9.cloned.1.call-update) | async-done | bytes 262160 | tf_op jit(solution)/shard_map/psum | solution.py:84
  324.6 1.1 fusion.522
  325.9 0.7 fusion.52
  326.6 0.7 fusion.54
  327.2 0.9 copy.111
  328.1 19.6 %all-reduce.11.cloned.1.call-done = f32[16,4096]{1,0:T(8,128)} async-done(((f32[16,4096]{1,0:T(8,128)}), f32[16,4096]{1,0:T(8,128)}) %all-reduce.11.cloned.1.call-update) | async-done | bytes 262160 | tf_op jit(solution)/shard_map/psum | solution.py:84
  347.7 1.1 fusion.524
  349.0 0.7 fusion.55
  349.7 4.9 %all_gather.3 = f32[4,8192]{1,0:T(4,128)S(1)} all-gather(f32[4,4096]{1,0:T(4,128)S(1)} %broadcast_divide_fusion), channel_id=1, replica_groups=mesh['groups'=2,'space'=4,'date'=2,'band'=2] {'date'}, dimensions={1}, use_global_device_ids=true | all-gather | bytes 196608 | tf_op jit(solution)/shard_map/all_gather | solution.py:141
  354.6 0.7 copy.115
  (217 shorter events, 13.9 us)
Async XLA Ops:
  6.5 151.0 %copy-start = (f32[1,128,128]{2,1,0:T(8,128)S(1)}, f32[1,128,128]{2,1,0:T(8,128)}, u32[]{:S(2)}) copy-start(f32[1,128,128]{2,1,0:T(8,128)} %param.15) | copy-start | bytes 196612
  7.9 16.5 %collective-permute-start = (f32[8,4,16,256]{3,2,0,1:T(8,128)S(1)}, f32[8,4,16,256]{3,2,0,1:T(8,128)S(1)}, u32[]{:S(2)}, u32[]{:S(2)}) collective-permute-start(f32[8,4,16,256]{3,2,0,1:T(8,128)S(1)} %get-tuple-element.111), channel_id=1, source_target_pairs={{0,4},{4,8},{8,12},{1,5},{5,9},{9,13},{2,6},{6,10},{10,14},{3,7},{... | collective-permute-start | bytes 1572872 | tf_op jit(solution)/shard_map/ppermute | solution.py:20
  12.9 15.3 %collective-permute-start.1 = (f32[8,4,16,256]{3,2,0,1:T(8,128)S(1)}, f32[8,4,16,256]{3,2,0,1:T(8,128)S(1)}, u32[]{:S(2)}, u32[]{:S(2)}) collective-permute-start(f32[8,4,16,256]{3,2,0,1:T(8,128)S(1)} %get-tuple-element.112), channel_id=1, source_target_pairs={{4,0},{8,4},{12,8},{5,1},{9,5},{13,9},{6,2},{10,6},{14,10},{7,3},{... | collective-permute-start | bytes 1572872 | tf_op jit(solution)/shard_map/ppermute | solution.py:23
  15.3 12.8 %copy-start.51 = (f32[32,64]{1,0:T(8,128)}, f32[32,64]{1,0:T(8,128)S(1)}, u32[]{:S(2)}) copy-start(f32[32,64]{1,0:T(8,128)S(1)} %get-tuple-element.130) | copy-start | bytes 24580
  15.3 12.8 %copy-start.53 = (f32[32,64]{1,0:T(8,128)}, f32[32,64]{1,0:T(8,128)S(1)}, u32[]{:S(2)}) copy-start(f32[32,64]{1,0:T(8,128)S(1)} %get-tuple-element.131) | copy-start | bytes 24580
  15.3 12.8 %copy-start.55 = (f32[32,64]{1,0:T(8,128)}, f32[32,64]{1,0:T(8,128)S(1)}, u32[]{:S(2)}) copy-start(f32[32,64]{1,0:T(8,128)S(1)} %get-tuple-element.132) | copy-start | bytes 24580
  15.4 12.8 %copy-start.57 = (f32[32,64]{1,0:T(8,128)}, f32[32,64]{1,0:T(8,128)S(1)}, u32[]{:S(2)}) copy-start(f32[32,64]{1,0:T(8,128)S(1)} %get-tuple-element.133) | copy-start | bytes 24580
  15.4 12.8 %copy-start.59 = (f32[32,64]{1,0:T(8,128)}, f32[32,64]{1,0:T(8,128)S(1)}, u32[]{:S(2)}) copy-start(f32[32,64]{1,0:T(8,128)S(1)} %get-tuple-element.134) | copy-start | bytes 24580
  15.4 12.8 %copy-start.61 = (f32[32,64]{1,0:T(8,128)}, f32[32,64]{1,0:T(8,128)S(1)}, u32[]{:S(2)}) copy-start(f32[32,64]{1,0:T(8,128)S(1)} %get-tuple-element.135) | copy-start | bytes 24580
  15.4 12.8 %copy-start.63 = (f32[32,64]{1,0:T(8,128)}, f32[32,64]{1,0:T(8,128)S(1)}, u32[]{:S(2)}) copy-start(f32[32,64]{1,0:T(8,128)S(1)} %get-tuple-element.136) | copy-start | bytes 24580
  22.2 34.7 %copy-start.3 = (f32[256,256]{1,0:T(8,128)}, f32[256,256]{1,0:T(8,128)S(1)}, u32[]{:S(2)}) copy-start(f32[256,256]{1,0:T(8,128)S(1)} %get-tuple-element.160) | copy-start | bytes 786436
  22.2 34.6 %copy-start.4 = (f32[256,256]{1,0:T(8,128)}, f32[256,256]{1,0:T(8,128)S(1)}, u32[]{:S(2)}) copy-start(f32[256,256]{1,0:T(8,128)S(1)} %get-tuple-element.161) | copy-start | bytes 786436
  22.2 34.6 %copy-start.5 = (f32[256,256]{1,0:T(8,128)}, f32[256,256]{1,0:T(8,128)S(1)}, u32[]{:S(2)}) copy-start(f32[256,256]{1,0:T(8,128)S(1)} %get-tuple-element.162) | copy-start | bytes 786436
  22.3 8.5 %copy-start.7 = (f32[256,256]{1,0:T(8,128)}, f32[256,256]{1,0:T(8,128)S(1)}, u32[]{:S(2)}) copy-start(f32[256,256]{1,0:T(8,128)S(1)} %get-tuple-element.164) | copy-start | bytes 786436
  22.3 34.6 %copy-start.6 = (f32[256,256]{1,0:T(8,128)}, f32[256,256]{1,0:T(8,128)S(1)}, u32[]{:S(2)}) copy-start(f32[256,256]{1,0:T(8,128)S(1)} %get-tuple-element.163) | copy-start | bytes 786436
  22.3 8.4 %copy-start.9 = (f32[256,256]{1,0:T(8,128)}, f32[256,256]{1,0:T(8,128)S(1)}, u32[]{:S(2)}) copy-start(f32[256,256]{1,0:T(8,128)S(1)} %get-tuple-element.165) | copy-start | bytes 786436
  22.4 8.4 %copy-start.11 = (f32[256,256]{1,0:T(8,128)}, f32[256,256]{1,0:T(8,128)S(1)}, u32[]{:S(2)}) copy-start(f32[256,256]{1,0:T(8,128)S(1)} %get-tuple-element.166) | copy-start | bytes 786436
  22.4 8.4 %copy-start.13 = (f32[256,256]{1,0:T(8,128)}, f32[256,256]{1,0:T(8,128)S(1)}, u32[]{:S(2)}) copy-start(f32[256,256]{1,0:T(8,128)S(1)} %get-tuple-element.167) | copy-start | bytes 786436
  22.4 8.4 %copy-start.15 = (f32[256,256]{1,0:T(8,128)}, f32[256,256]{1,0:T(8,128)S(1)}, u32[]{:S(2)}) copy-start(f32[256,256]{1,0:T(8,128)S(1)} %get-tuple-element.168) | copy-start | bytes 786436
  22.5 8.4 %copy-start.17 = (f32[256,256]{1,0:T(8,128)}, f32[256,256]{1,0:T(8,128)S(1)}, u32[]{:S(2)}) copy-start(f32[256,256]{1,0:T(8,128)S(1)} %get-tuple-element.169) | copy-start | bytes 786436
  22.5 8.4 %copy-start.19 = (f32[256,256]{1,0:T(8,128)}, f32[256,256]{1,0:T(8,128)S(1)}, u32[]{:S(2)}) copy-start(f32[256,256]{1,0:T(8,128)S(1)} %get-tuple-element.170) | copy-start | bytes 786436
  22.5 8.3 %copy-start.21 = (f32[256,256]{1,0:T(8,128)}, f32[256,256]{1,0:T(8,128)S(1)}, u32[]{:S(2)}) copy-start(f32[256,256]{1,0:T(8,128)S(1)} %get-tuple-element.171) | copy-start | bytes 786436
  22.5 8.3 %copy-start.23 = (f32[256,256]{1,0:T(8,128)}, f32[256,256]{1,0:T(8,128)S(1)}, u32[]{:S(2)}) copy-start(f32[256,256]{1,0:T(8,128)S(1)} %get-tuple-element.172) | copy-start | bytes 786436
  22.6 8.3 %copy-start.25 = (f32[256,256]{1,0:T(8,128)}, f32[256,256]{1,0:T(8,128)S(1)}, u32[]{:S(2)}) copy-start(f32[256,256]{1,0:T(8,128)S(1)} %get-tuple-element.173) | copy-start | bytes 786436
  22.6 8.3 %copy-start.27 = (f32[256,256]{1,0:T(8,128)}, f32[256,256]{1,0:T(8,128)S(1)}, u32[]{:S(2)}) copy-start(f32[256,256]{1,0:T(8,128)S(1)} %get-tuple-element.174) | copy-start | bytes 786436
  22.7 8.2 %copy-start.29 = (f32[256,256]{1,0:T(8,128)}, f32[256,256]{1,0:T(8,128)S(1)}, u32[]{:S(2)}) copy-start(f32[256,256]{1,0:T(8,128)S(1)} %get-tuple-element.175) | copy-start | bytes 786436
  22.7 8.2 %copy-start.31 = (f32[256,256]{1,0:T(8,128)}, f32[256,256]{1,0:T(8,128)S(1)}, u32[]{:S(2)}) copy-start(f32[256,256]{1,0:T(8,128)S(1)} %get-tuple-element.176) | copy-start | bytes 786436
  22.8 8.2 %copy-start.33 = (f32[256,256]{1,0:T(8,128)}, f32[256,256]{1,0:T(8,128)S(1)}, u32[]{:S(2)}) copy-start(f32[256,256]{1,0:T(8,128)S(1)} %get-tuple-element.177) | copy-start | bytes 786436
  35.6 13.4 %collective-permute-start.2 = (f32[8,4,16,256]{3,2,0,1:T(8,128)S(1)}, f32[8,4,16,256]{3,2,0,1:T(8,128)}, u32[]{:S(2)}, u32[]{:S(2)}) collective-permute-start(f32[8,4,16,256]{3,2,0,1:T(8,128)S(1)} %get-tuple-element.109), channel_id=1, source_target_pairs={{0,4},{4,8},{8,12},{1,5},{5,9},{9,13},{2,6},{6,10},{10,14},{3,7},{... | collective-permute-start | bytes 1572872 | tf_op jit(solution)/shard_map/ppermute | solution.py:20
  39.8 14.2 %collective-permute-start.3 = (f32[8,4,16,256]{3,2,0,1:T(8,128)S(1)}, f32[8,4,16,256]{3,2,0,1:T(8,128)}, u32[]{:S(2)}, u32[]{:S(2)}) collective-permute-start(f32[8,4,16,256]{3,2,0,1:T(8,128)S(1)} %get-tuple-element.110), channel_id=1, source_target_pairs={{4,0},{8,4},{12,8},{5,1},{9,5},{13,9},{6,2},{10,6},{14,10},{7,3},{... | collective-permute-start | bytes 1572872 | tf_op jit(solution)/shard_map/ppermute | solution.py:23
  41.5 15.4 %copy-start.8 = (f32[256,256]{1,0:T(8,128)S(1)}, f32[256,256]{1,0:T(8,128)}, u32[]{:S(2)}) copy-start(f32[256,256]{1,0:T(8,128)} %copy-done.7) | copy-start | bytes 786436
  41.5 15.4 %copy-start.10 = (f32[256,256]{1,0:T(8,128)S(1)}, f32[256,256]{1,0:T(8,128)}, u32[]{:S(2)}) copy-start(f32[256,256]{1,0:T(8,128)} %copy-done.9) | copy-start | bytes 786436
  41.5 15.4 %copy-start.12 = (f32[256,256]{1,0:T(8,128)S(1)}, f32[256,256]{1,0:T(8,128)}, u32[]{:S(2)}) copy-start(f32[256,256]{1,0:T(8,128)} %copy-done.11) | copy-start | bytes 786436
  41.5 15.4 %copy-start.14 = (f32[256,256]{1,0:T(8,128)S(1)}, f32[256,256]{1,0:T(8,128)}, u32[]{:S(2)}) copy-start(f32[256,256]{1,0:T(8,128)} %copy-done.13) | copy-start | bytes 786436
  41.5 15.4 %copy-start.16 = (f32[256,256]{1,0:T(8,128)S(1)}, f32[256,256]{1,0:T(8,128)}, u32[]{:S(2)}) copy-start(f32[256,256]{1,0:T(8,128)} %copy-done.15) | copy-start | bytes 786436
  41.5 15.4 %copy-start.18 = (f32[256,256]{1,0:T(8,128)S(1)}, f32[256,256]{1,0:T(8,128)}, u32[]{:S(2)}) copy-start(f32[256,256]{1,0:T(8,128)} %copy-done.17) | copy-start | bytes 786436
  41.5 15.4 %copy-start.20 = (f32[256,256]{1,0:T(8,128)S(1)}, f32[256,256]{1,0:T(8,128)}, u32[]{:S(2)}) copy-start(f32[256,256]{1,0:T(8,128)} %copy-done.19) | copy-start | bytes 786436
  41.5 15.4 %copy-start.22 = (f32[256,256]{1,0:T(8,128)S(1)}, f32[256,256]{1,0:T(8,128)}, u32[]{:S(2)}) copy-start(f32[256,256]{1,0:T(8,128)} %copy-done.21) | copy-start | bytes 786436
  41.5 15.4 %copy-start.24 = (f32[256,256]{1,0:T(8,128)S(1)}, f32[256,256]{1,0:T(8,128)}, u32[]{:S(2)}) copy-start(f32[256,256]{1,0:T(8,128)} %copy-done.23) | copy-start | bytes 786436
  41.5 15.4 %copy-start.26 = (f32[256,256]{1,0:T(8,128)S(1)}, f32[256,256]{1,0:T(8,128)}, u32[]{:S(2)}) copy-start(f32[256,256]{1,0:T(8,128)} %copy-done.25) | copy-start | bytes 786436
  41.6 15.4 %copy-start.28 = (f32[256,256]{1,0:T(8,128)S(1)}, f32[256,256]{1,0:T(8,128)}, u32[]{:S(2)}) copy-start(f32[256,256]{1,0:T(8,128)} %copy-done.27) | copy-start | bytes 786436
  41.6 15.4 %copy-start.30 = (f32[256,256]{1,0:T(8,128)S(1)}, f32[256,256]{1,0:T(8,128)}, u32[]{:S(2)}) copy-start(f32[256,256]{1,0:T(8,128)} %copy-done.29) | copy-start | bytes 786436
  41.6 15.4 %copy-start.32 = (f32[256,256]{1,0:T(8,128)S(1)}, f32[256,256]{1,0:T(8,128)}, u32[]{:S(2)}) copy-start(f32[256,256]{1,0:T(8,128)} %copy-done.31) | copy-start | bytes 786436
  41.6 15.4 %copy-start.34 = (f32[256,256]{1,0:T(8,128)S(1)}, f32[256,256]{1,0:T(8,128)}, u32[]{:S(2)}) copy-start(f32[256,256]{1,0:T(8,128)} %copy-done.33) | copy-start | bytes 786436
  41.6 15.4 %copy-start.36 = (f32[256,256]{1,0:T(8,128)S(1)}, f32[256,256]{1,0:T(8,128)}, u32[]{:S(2)}) copy-start(f32[256,256]{1,0:T(8,128)} %copy-done.35) | copy-start | bytes 786436
  63.3 15.9 %copy-start.52 = (f32[32,64]{1,0:T(8,128)S(1)}, f32[32,64]{1,0:T(8,128)}, u32[]{:S(2)}) copy-start(f32[32,64]{1,0:T(8,128)} %copy-done.51) | copy-start | bytes 24580
  63.3 15.9 %copy-start.54 = (f32[32,64]{1,0:T(8,128)S(1)}, f32[32,64]{1,0:T(8,128)}, u32[]{:S(2)}) copy-start(f32[32,64]{1,0:T(8,128)} %copy-done.53) | copy-start | bytes 24580
  63.3 15.9 %copy-start.56 = (f32[32,64]{1,0:T(8,128)S(1)}, f32[32,64]{1,0:T(8,128)}, u32[]{:S(2)}) copy-start(f32[32,64]{1,0:T(8,128)} %copy-done.55) | copy-start | bytes 24580
  63.3 15.9 %copy-start.58 = (f32[32,64]{1,0:T(8,128)S(1)}, f32[32,64]{1,0:T(8,128)}, u32[]{:S(2)}) copy-start(f32[32,64]{1,0:T(8,128)} %copy-done.57) | copy-start | bytes 24580
  63.3 15.9 %copy-start.60 = (f32[32,64]{1,0:T(8,128)S(1)}, f32[32,64]{1,0:T(8,128)}, u32[]{:S(2)}) copy-start(f32[32,64]{1,0:T(8,128)} %copy-done.59) | copy-start | bytes 24580
  63.3 15.9 %copy-start.62 = (f32[32,64]{1,0:T(8,128)S(1)}, f32[32,64]{1,0:T(8,128)}, u32[]{:S(2)}) copy-start(f32[32,64]{1,0:T(8,128)} %copy-done.61) | copy-start | bytes 24580
  63.3 15.9 %copy-start.64 = (f32[32,64]{1,0:T(8,128)S(1)}, f32[32,64]{1,0:T(8,128)}, u32[]{:S(2)}) copy-start(f32[32,64]{1,0:T(8,128)} %copy-done.63) | copy-start | bytes 24580
  63.4 11.5 %collective-permute-start.4 = (f32[8,4,16,256]{3,2,0,1:T(8,128)S(1)}, f32[8,4,16,256]{3,2,0,1:T(8,128)S(1)}, u32[]{:S(2)}, u32[]{:S(2)}) collective-permute-start(f32[8,4,16,256]{3,2,0,1:T(8,128)S(1)} %get-tuple-element.107), channel_id=1, source_target_pairs={{0,4},{4,8},{8,12},{1,5},{5,9},{9,13},{2,6},{6,10},{10,14},{3,7},{... | collective-permute-start | bytes 1572872 | tf_op jit(solution)/shard_map/ppermute | solution.py:20
  66.2 13.0 %collective-permute-start.5 = (f32[8,4,16,256]{3,2,0,1:T(8,128)S(1)}, f32[8,4,16,256]{3,2,0,1:T(8,128)}, u32[]{:S(2)}, u32[]{:S(2)}) collective-permute-start(f32[8,4,16,256]{3,2,0,1:T(8,128)S(1)} %get-tuple-element.108), channel_id=1, source_target_pairs={{4,0},{8,4},{12,8},{5,1},{9,5},{13,9},{6,2},{10,6},{14,10},{7,3},{... | collective-permute-start | bytes 1572872 | tf_op jit(solution)/shard_map/ppermute | solution.py:23
  68.3 25.0 %all-to-all-start.2 = ((f32[4,1,8]{2,1,0:T(1,128)}), f32[4,1,8]{2,1,0:T(1,128)S(1)}, u32[]{:S(2)}, u32[]{:S(2)}) async-start(f32[4,1,8]{2,1,0:T(1,128)} %bitcast.43), calls=%async_computation.2 | async-start | bytes 4096 | tf_op jit(solution)/shard_map/all_to_all | solution.py:122
  93.3 60.3 %copy-start.65 = (f32[1,4,4]{2,1,0:T(4,128)S(1)}, f32[1,4,4]{2,1,0:T(4,128)}, u32[]{:S(2)}) copy-start(f32[1,4,4]{2,1,0:T(4,128)} %param.14) | copy-start | bytes 196
  93.3 50.6 %all-to-all-start.1 = ((f32[4,8,8,4,4,128]{5,1,4,3,2,0:T(8,128)}), f32[4,8,8,4,4,128]{5,1,4,3,2,0:T(8,128)S(1)}, u32[]{:S(2)}, u32[]{:S(2)}) async-start(f32[4,8,8,4,4,128]{5,1,4,3,2,0:T(8,128)} %fusion.56), calls=%async_computation.1 | async-start | bytes 4194304 | tf_op jit(solution)/shard_map/all_to_all | solution.py:121
  144.5 53.8 %all-to-all-start = ((f32[8,1,2]{0,1,2:T(1,128)}), f32[8,1,2]{0,1,2:T(1,128)S(1)}, u32[]{:S(2)}, u32[]{:S(2)}) async-start(f32[8,1,2]{0,1,2:T(1,128)} %broadcast_in_dim.5), calls=%async_computation | async-start | bytes 2048 | tf_op jit(solution)/shard_map/all_to_all | solution.py:138
  198.3 14.2 %all-to-all-start.3 = ((f32[2,1,131072]{2,1,0:T(1,128)}), f32[2,1,131072]{2,1,0:T(1,128)S(1)}, u32[]{:S(2)}, u32[]{:S(2)}) async-start(f32[2,1,131072]{2,1,0:T(1,128)} %reshape.1121), calls=%async_computation.3 | async-start | bytes 2097152 | tf_op jit(solution)/shard_map/all_to_all | solution.py:137
  201.9 76.5 %all-reduce.5.cloned.1.call-start = ((), (), s32[]{:S(2)}) async-start(), calls=%async_computation.4 | async-start | bytes 524288 | tf_op jit(solution)/shard_map/psum | solution.py:84
  259.1 42.4 %all-reduce.7.cloned.1.call-start = ((), (), s32[]{:S(2)}) async-start(), calls=%async_computation.5 | async-start | bytes 524288 | tf_op jit(solution)/shard_map/psum | solution.py:84
  281.9 42.7 %all-reduce.9.cloned.1.call-start = ((), (), s32[]{:S(2)}) async-start(), calls=%async_computation.6 | async-start | bytes 524288 | tf_op jit(solution)/shard_map/psum | solution.py:84
  305.0 42.7 %all-reduce.11.cloned.1.call-start = ((), (), s32[]{:S(2)}) async-start(), calls=%async_computation.7 | async-start | bytes 524288 | tf_op jit(solution)/shard_map/psum | solution.py:84
  326.6 28.7 %copy-start.1 = (f32[1,128,128]{2,1,0:T(8,128)S(1)}, f32[1,128,128]{2,1,0:T(8,128)}, u32[]{:S(2)}) copy-start(f32[1,128,128]{2,1,0:T(8,128)} %param.15) | copy-start | bytes 196612
  (20 other events, 137.7 us)
Sparse Core Ops, SparseCore 0:
  259.2 19.1 all-reduce.4
  282.0 19.4 all-reduce.6
  305.1 19.4 all-reduce.8
  328.2 19.4 all-reduce.10
where the time goes:
time: 369 us; the launch traced here: 362 us
  waiting for transfers between devices  108 us (29%)
  local copies, waits for them, and re-layouts  89.1 us (24%)
  blocking collectives  50.4 us (14%)
  starting transfers between devices  37.3 us (10%)
  matrix products  36.9 us (10%)
  other arithmetic  24.6 us (7%)
  between operations  15.8 us (4%)
    psum x4, waiting for transfers between devices, band_total(): return lax.psum(squares, 'band')  77.5 us
    unnamed x143, local copies, waits for them, and re-layouts  55.2 us
    psum x1, blocking collectives, local(): count_sum = lax.psum(count_part, ('space', 'date'))  45.5 us
    dot_general x3, matrix products, correct_strip(): jnp.einsum('tbrj,bcj->tbrc', row_pass, column_matrix, precision=highest)  18 us
    all_to_all x2, local copies, waits for them, and re-layouts, local(): lax.all_to_all(stacked, 'date', split_axis=2, concat_axis=0, tiled=True)  13.7 us
    ppermute x3, waiting for transfers between devices, padded_2(): lax.ppermute(lax.slice_in_dim(block, 0, width, axis=dim), axis, backward)  13 us
    ppermute x3, starting transfers between devices, padded_2(): lax.ppermute(lax.slice_in_dim(block, block.shape[dim] - width, None, axis...  12 us
    all_to_all x1, waiting for transfers between devices, local(): lax.all_to_all(stacked, 'date', split_axis=2, concat_axis=0, tiled=True)  9.67 us
  transfers between devices with their start and end apart: 14, of which 10 were waited for; matrix products, arithmetic and copies ran while one was open for 20% of the time, Pallas kernels for 0%

commit v1 on v0

v1 whole, which is shorter than its diff:
```python
import functools
import jax
import jax.numpy as jnp
from jax import lax
from jax.experimental import pallas as pl
from jax.experimental.pallas import tpu as pltpu
from jax.sharding import PartitionSpec as P

BROWS = 4
BCOLS = 128
ITERS = 4
MESH = pl.DeviceIdType.MESH
smooth_sq = 0.01
f32 = jnp.float32
bf16 = jnp.bfloat16


def split(value):
    high = value.astype(bf16)
    return high, (value - high.astype(f32)).astype(bf16)


def dot3(left, right):
    lh, ll = left
    rh, rl = right
    d = functools.partial(jnp.dot, preferred_element_type=f32)
    return d(lh, rh) + (d(ll, rh) + d(lh, rl))


def toeplitz(row, size, radius):
    base = jnp.broadcast_to(row, (8, size))
    base = pltpu.roll(base, size - radius, 1)
    sub = lax.broadcasted_iota(jnp.int32, (8, size), 0)
    for bit in (1, 2, 4):
        base = jnp.where((sub & bit) != 0, pltpu.roll(base, bit, 1), base)
    gap = lax.broadcasted_iota(jnp.int32, (8, size), 1) - sub
    parts = []
    for start in range(0, size, 8):
        turned = base if start == 0 else pltpu.roll(base, start, 1)
        near = jnp.abs(gap - start) <= radius
        parts.append(jnp.where(near, turned, 0.0))
    return jnp.concatenate(parts, axis=0)


def kernel(
    dims, x_ref, meta_ref, taps_ref, strength_ref, cols_ref, out_ref,
    grid, row_h, row_l, col_h, col_l, meta_all, place_h, place_l, asm, stack, est, res,
    msend, mrecv, gsend, grecv, ssend, srecv, esend, erecv,
):
    S, D, C, T, B, RS, W, PASSES, radius, ppd, nch = dims
    n = S * D * C
    rows = S * RS
    nb = min(B, ppd)
    cp = ppd // nch
    share = asm.shape[2]
    s = lax.axis_index("space")
    d = lax.axis_index("date")
    c = lax.axis_index("band")
    me = (s * D + d) * C + c
    dc = d * C + c
    q0 = s * ppd

    def where_is(index):
        return {
            "space": index // (D * C),
            "date": lax.rem(index // C, D),
            "band": lax.rem(index, C),
        }

    barrier = pltpu.get_barrier_semaphore()

    def greet(k, carry):
        other = lax.rem(me + k, n)
        pl.semaphore_signal(barrier, inc=1, device_id=where_is(other), device_id_type=MESH)
        return carry

    lax.fori_loop(1, n, greet, 0)
    pl.semaphore_wait(barrier, n - 1)

    md = s * D + d

    def meta_copy(to, slot, sem):
        return pltpu.make_async_remote_copy(
            src_ref=meta_ref,
            dst_ref=meta_all.at[slot],
            send_sem=msend.at[to],
            recv_sem=mrecv.at[sem],
            device_id={"space": to // D, "date": lax.rem(to, D)},
            device_id_type=MESH,
        )

    def meta_start(k, carry):
        meta_copy(lax.rem(md + k, S * D), md, md).start()
        return carry

    lax.fori_loop(1, S * D, meta_start, 0)
    meta_all[md] = meta_ref[...]

    def grid_copy(other, chunk, at):
        return pltpu.make_async_remote_copy(
            src_ref=x_ref.at[pl.ds(other * ppd + chunk * cp, cp)],
            dst_ref=grid.at[pl.ds(chunk * cp, cp), pl.ds(pl.multiple_of(at * RS, RS), RS)],
            send_sem=gsend.at[other, chunk],
            recv_sem=grecv.at[at, chunk],
            device_id={"space": other},
            device_id_type=MESH,
        )

    for chunk in range(nch):

        def grid_start(k, carry, chunk=chunk):
            grid_copy(lax.rem(s + k, S), chunk, s).start()
            return carry

        lax.fori_loop(1, S, grid_start, 0)
    grid[:, pl.ds(pl.multiple_of(s * RS, RS), RS), :] = x_ref[pl.ds(q0, ppd)]

    def build(index, carry):
        which = index // nb
        local_band = lax.rem(index, nb)
        band = lax.rem(q0 + local_band, B)
        both = taps_ref[which * B + band]
        both = both / jnp.sum(both, axis=1, keepdims=True)
        high, low = split(toeplitz(both[0:1, :rows], rows, radius))
        row_h[index] = high
        row_l[index] = low
        high, low = split(toeplitz(both[1:2, :W], W, radius))
        col_h[index] = high
        col_l[index] = low
        return carry

    lax.fori_loop(0, PASSES * nb, build, 0)

    def meta_wait(k, carry):
        other = lax.rem(md + k, S * D)
        copy = meta_copy(other, other, other)
        copy.wait_send()
        copy.wait_recv()
        return carry

    lax.fori_loop(1, S * D, meta_wait, 0)

    tile_rows = share * D * C
    pieces = [meta_all[i * D + d, 0:8, :] for i in range(S)]
    total = pieces[0]
    for piece in pieces[1:]:
        total = total + piece
    map_row = lax.broadcasted_iota(jnp.int32, (S * tile_rows, rows), 0)
    for half in range(2):
        target = total[half : half + 1]
        first = total[2 + half : 3 + half].astype(jnp.int32)
        behind = map_row - first
        place = jnp.zeros((S * tile_rows, rows), f32)
        for i in range(BROWS):
            value = jnp.zeros((1, rows), f32)
            for tile in range(S):
                value = value + jnp.where(target == tile, pieces[tile][4 + i : 5 + i], 0.0)
            place = jnp.where(behind == i, value, place)
        high, low = split(place)
        place_h[half] = high
        place_l[half] = low

    def share_copy(other, source, chunk):
        sd = lax.rem(source // C, D)
        sc = lax.rem(source, C)
        ss = source // (D * C)
        return pltpu.make_async_remote_copy(
            src_ref=asm.at[other, pl.ds(chunk * cp, cp)],
            dst_ref=stack.at[sd, sc, pl.ds(ss * ppd + chunk * cp, cp)],
            send_sem=ssend.at[other, chunk],
            recv_sem=srecv.at[source, chunk],
            device_id=where_is(other),
            device_id_type=MESH,
        )

    def chunk_step(chunk, carry):
        def grid_wait(k, inner):
            other = lax.rem(s + k, S)
            grid_copy(other, chunk, other).wait_recv()
            return inner

        lax.fori_loop(1, S, grid_wait, 0)
        for j in range(cp):
            plane = chunk * cp + j
            local_band = lax.rem(plane, nb)
            band = lax.rem(q0 + plane, B)
            value = grid[plane]
            for which in range(PASSES):
                index = which * nb + local_band
                mid = dot3((row_h[index], row_l[index]), split(value))
                blurred = dot3(split(mid), (col_h[index], col_l[index]))
                value = value + strength_ref[which, band] * (value - blurred)
            vh, vl = split(value)
            laid = dot3((place_h[0], place_l[0]), (vh[:, :BCOLS], vl[:, :BCOLS]))
            laid = laid + dot3((place_h[1], place_l[1]), (vh[:, BCOLS:], vl[:, BCOLS:]))
            asm[:, plane] = laid.reshape(n, share, BCOLS)

        def share_start(k, inner):
            share_copy(lax.rem(me + k, n), me, chunk).start()
            return inner

        lax.fori_loop(1, n, share_start, 0)
        return carry

    lax.fori_loop(0, nch, chunk_step, 0)
    stack[d, c, pl.ds(q0, ppd)] = asm[me]

    col_pair = split(cols_ref[...])

    def resample(source):
        sd = lax.rem(source // C, D)
        sc = lax.rem(source, C)
        ss = source // (D * C)
        block = stack[sd, sc, pl.ds(ss * ppd, ppd)].reshape(ppd * share, BCOLS)
        done = dot3(split(block), col_pair)
        stack[sd, sc, pl.ds(ss * ppd, ppd)] = done.reshape(ppd, share, BCOLS)

    resample(me)

    def share_wait(k, carry):
        source = lax.rem(me + n - k, n)

        def one(chunk, inner):
            share_copy(me, source, chunk).wait_recv()
            return inner

        lax.fori_loop(0, nch, one, 0)
        resample(source)
        return carry

    lax.fori_loop(1, n, share_wait, 0)

    count_sum = jnp.zeros((1, BCOLS), f32)
    for i in range(S * D):
        count_sum = count_sum + jnp.sum(meta_all[i, 8 : 8 + T, :BCOLS], axis=0, keepdims=True)
    mean_count = count_sum / (T * D * S)
    weights = []
    for i in range(D):
        mine = meta_all[s * D + i, 8 : 8 + T, :BCOLS]
        weights.append(mine / (mine + mean_count))

    step = 8 if share % 8 == 0 else share
    for start in range(0, share, step):

        def picked(i, t):
            return stack[i, :, t * B : (t + 1) * B, start : start + step, :]

        def weighted(estimate):
            num = jnp.zeros((C, B, step, BCOLS), f32)
            den = jnp.zeros((step, BCOLS), f32)
            for i in range(D):
                for t in range(T):
                    part = picked(i, t)
                    weight = jnp.broadcast_to(weights[i][t : t + 1], (step, BCOLS))
                    if estimate is not None:
                        away = part - estimate
                        square = jnp.sum(jnp.sum(away * away, axis=0), axis=0)
                        weight = weight * lax.rsqrt(square + smooth_sq)
                    num = num + weight * part
                    den = den + weight
            return num / den

        estimate = weighted(None)
        estimate = lax.fori_loop(0, ITERS, lambda _, e: weighted(e), estimate)
        est[:, :, start : start + step, :] = estimate

    def est_copy(other, source):
        return pltpu.make_async_remote_copy(
            src_ref=est.at[lax.rem(other, C)],
            dst_ref=res.at[source],
            send_sem=esend.at[other],
            recv_sem=erecv.at[source],
            device_id={"date": other // C, "band": lax.rem(other, C)},
            device_id_type=MESH,
        )

    def est_start(k, carry):
        est_copy(lax.rem(dc + k, D * C), dc).start()
        return carry

    lax.fori_loop(1, D * C, est_start, 0)
    res[dc] = est[c]

    def est_wait(k, carry):
        other = lax.rem(dc + k, D * C)
        copy = est_copy(other, other)
        copy.wait_send()
        copy.wait_recv()
        return carry

    lax.fori_loop(1, D * C, est_wait, 0)
    for i in range(D * C):
        out_ref[:, i * share : (i + 1) * share, :] = res[i]

    def chunk_end(chunk, carry):
        def grid_end(k, inner):
            grid_copy(lax.rem(s + k, S), chunk, s).wait_send()
            return inner

        def share_end(k, inner):
            share_copy(lax.rem(me + k, n), me, chunk).wait_send()
            return inner

        lax.fori_loop(1, S, grid_end, 0)
        lax.fori_loop(1, n, share_end, 0)
        return carry

    lax.fori_loop(0, nch, chunk_end, 0)


def local(
    reflect, kernels, strength, destinations, offsets, counts, resample_rows, resample_columns
):
    S, D, C = lax.axis_size("space"), lax.axis_size("date"), lax.axis_size("band")
    T, B, RS, W = reflect.shape
    PASSES, _, tap_count = kernels.shape
    radius = (tap_count - 1) // 2
    rows = S * RS
    n = S * D * C
    ppd = T * B // S
    nch = min(4, ppd)
    nb = min(B, ppd)
    tile_rows = destinations.shape[0] * BROWS
    share = tile_rows // (D * C)
    s = lax.axis_index("space")

    target = destinations[:, 0].reshape(-1, 2).T
    first = target * tile_rows + offsets.reshape(-1, 2).T
    places = jnp.repeat(jnp.concatenate([target, first]), BROWS, axis=1)
    strip = jnp.arange(rows)[None, :] // RS == s
    places = jnp.where(strip, jnp.tile(places, (1, S)), 0).astype(f32)
    tiled_rows = jnp.tile(resample_rows[0], (1, rows // BROWS))
    meta = jnp.concatenate(
        [places, tiled_rows, jnp.broadcast_to(counts.astype(f32), (T, rows))]
    )
    width = max(W, rows)
    taps = jnp.stack([kernels, kernels[:, :, ::-1]], axis=2).reshape(PASSES * B, 2, tap_count)
    taps = jnp.pad(taps, ((0, 0), (0, 0), (0, width - tap_count)))

    dims = (S, D, C, T, B, RS, W, PASSES, radius, ppd, nch)
    vmem = pl.BlockSpec(memory_space=pltpu.VMEM)
    smem = pl.BlockSpec(memory_space=pltpu.SMEM)
    dma = pltpu.SemaphoreType.DMA
    return pl.pallas_call(
        functools.partial(kernel, dims),
        out_shape=jax.ShapeDtypeStruct((B, tile_rows, BCOLS), f32),
        in_specs=[vmem, vmem, vmem, smem, vmem],
        out_specs=vmem,
        scratch_shapes=[
            pltpu.VMEM((ppd, rows, W), f32),
            pltpu.VMEM((PASSES * nb, rows, rows), bf16),
            pltpu.VMEM((PASSES * nb, rows, rows), bf16),
            pltpu.VMEM((PASSES * nb, W, W), bf16),
            pltpu.VMEM((PASSES * nb, W, W), bf16),
            pltpu.VMEM((S * D, 8 + T, rows), f32),
            pltpu.VMEM((2, S * tile_rows, rows), bf16),
            pltpu.VMEM((2, S * tile_rows, rows), bf16),
            pltpu.VMEM((n, ppd, share, BCOLS), f32),
            pltpu.VMEM((D, C, T * B, share, BCOLS), f32),
            pltpu.VMEM((C, B, share, BCOLS), f32),
            pltpu.VMEM((D * C, B, share, BCOLS), f32),
            dma((S * D,)),
            dma((S * D,)),
            dma((S, nch)),
            dma((S, nch)),
            dma((n, nch)),
            dma((n, nch)),
            dma((D * C,)),
            dma((D * C,)),
        ],
        compiler_params=pltpu.CompilerParams(
            collective_id=0, has_side_effects=True, vmem_limit_bytes=56 * 1024 * 1024
        ),
    )(reflect.reshape(T * B, RS, W), meta, taps, strength, resample_columns[0])


def solution(mesh):
    in_specs = (
        P("date", "band", ("groups", "space"), None),
        P(None, "band", None),
        P(None, "band"),
        P(("groups", "space"), None),
        P(("groups", "space")),
        P("date", ("groups", "space")),
        P(("groups", "space"), None, None),
        P(("groups", "space"), None, None),
    )
    out_specs = P("band", ("groups", "space"), None)
    return jax.shard_map(local, mesh=mesh, in_specs=in_specs, out_specs=out_specs, check_vma=False)
```

time: 369 us -> 69.9 us (0.19); the launches traced: 362 us -> 69.6 us
  waiting for transfers between devices: 108 us -> 0 us
  local copies, waits for them, and re-layouts: 89.1 us -> 4.96 us
  Pallas kernels: 0 us -> 62.5 us
  blocking collectives: 50.4 us -> 0 us
  starting transfers between devices: 37.3 us -> 0 us
  matrix products: 36.9 us -> 0 us
  other arithmetic: 24.6 us -> 2.07 us
  between operations: 15.8 us -> 0.03 us
    psum x4 -> x0, waiting for transfers between devices: 77.5 us -> none  [band_total(): return lax.psum(squares, 'band')]
    pallas_call x0 -> x1, Pallas kernels: none -> 62.5 us  [local(): pl.pallas_call(functools.partial(kernel, dims), out_shape=jax.ShapeDtypeS...]
    unnamed x143 -> x12, local copies, waits for them, and re-layouts: 55.2 us -> 4.2 us
    psum x1 -> x0, blocking collectives: 45.5 us -> none  [local(): count_sum = lax.psum(count_part, ('space', 'date'))]
    dot_general x11 -> x0, matrix products: 36.9 us -> none  [the longest x3 18 us: correct_strip(): jnp.einsum('tbrj,bcj->tbrc', row_pass, column_matrix, precision=highest)]
    ppermute x6 -> x0, waiting for transfers between devices: 20.9 us -> none  [the longest x3 13 us: padded_2(): lax.ppermute(lax.slice_in_dim(block, 0, width, axis=dim), axis, backward)]
    all_to_all x4 -> x0, starting transfers between devices: 20.6 us -> none  [the longest x1 9.11 us: local(): lax.all_to_all(spread, 'date', split_axis=2, concat_axis=0, tiled=True)]
    ppermute x6 -> x0, starting transfers between devices: 16 us -> none  [the longest x3 12 us: padded_2(): lax.ppermute(lax.slice_in_dim(block, block.shape[dim] - width, None, axis...]
  transfers between devices with their start and end apart: 14 -> 0, of which waited for: 10 -> 0; matrix products, arithmetic and copies ran while one was open for 20% -> 0% of each run, Pallas kernels for 0% -> 0%
where the time goes in v1:
time: 69.9 us; the launch traced here: 69.6 us
  Pallas kernels  62.5 us (89%)
  local copies, waits for them, and re-layouts  4.96 us (7%)
  other arithmetic  2.07 us (3%)
    pallas_call x1, Pallas kernels, local(): pl.pallas_call(functools.partial(kernel, dims), out_shape=jax.ShapeDtypeS...  62.5 us
    unnamed x12, local copies, waits for them, and re-layouts  4.2 us

profile of v1, /device:TPU:0, one launch (start us, length us, event | category | flops | bytes accessed | tf_op | source)
XLA Modules:
  0.0 69.6 jit_solution(8181818006402585319)
XLA Ops:
  0.0 0.0 copy-start.3
  0.0 0.5 broadcast.63
  0.5 0.1 copy-done.3
  0.7 0.7 reduce.3
  1.3 0.0 copy-start.4
  1.3 0.6 copy-done.4
  2.0 0.1 pad.9.clone
  2.1 0.1 reshape_squeeze.3
  2.1 0.0 copy-start.2
  2.1 0.7 copy-done.2
  2.8 0.1 reshape.59
  2.9 0.1 pad_add_fusion
  3.0 0.0 copy-start
  3.0 0.1 copy.10
  3.0 0.6 copy-done
  3.7 0.1 rev.3
  3.8 0.1 broadcast_in_dim.24
  3.8 0.1 tile.20
  3.9 0.1 tile.22
  4.0 0.0 copy-start.1
  4.0 0.6 select_maximum_fusion.taps_ref
  4.6 0.1 copy-done.1
  4.7 0.1 tile.25
  4.8 0.7 maximum_maximum_fusion.meta_ref
  5.5 62.5 %shard_map.82 = f32[4,64,128]{2,1,0:T(8,128)} custom-call(f32[32,32,256]{2,1,0:T(8,128)} %bitcast.12, f32[16,128]{1,0:T(8,128)} %maximum_maximum_fusion.meta_ref, f32[12,2,256]{2,1,0:T(2,128)} %select_maximum_fusion.taps_ref, f32[3,4]{1,0:T(4,128)} %strength_ref.1, f32[128,128]{1,0:T(8,128)} %bitcast.13), custom_call_target="tpu_custom_call" | custom-call | tf_op jit(solution)/shard_map/pallas_call | solution.py:344
  68.0 1.6 %copy.12 = f32[4,64,128]{2,1,0:T(8,128)} copy(f32[4,64,128]{2,1,0:T(8,128)} %shard_map.82) | data formatting | bytes 262144
  (6 shorter events, 0.0 us)
Async XLA Ops:
  0.0 0.7 copy-start.3
  1.3 0.7 copy-start.4
  2.1 0.7 copy-start.2
  3.0 0.7 %copy-start = (f32[3,4,33]{2,1,0:T(4,128)S(1)}, f32[3,4,33]{2,1,0:T(4,128)}, u32[]{:S(2)}) copy-start(f32[3,4,33]{2,1,0:T(4,128)} %param.9) | copy-start | bytes 4756
  4.0 0.7 copy-start.1

commit v2 on v1

--- a/solution.py
+++ b/solution.py
@@ -318,7 +318,7 @@
     rows = S * RS
     n = S * D * C
     ppd = T * B // S
-    nch = min(4, ppd)
+    nch = min(2, ppd)
     nb = min(B, ppd)
     tile_rows = destinations.shape[0] * BROWS
     share = tile_rows // (D * C)

time: 69.9 us -> 67.3 us (0.963); the launches traced: 69.6 us -> 66.1 us
  Pallas kernels: 62.5 us -> 59.1 us
    pallas_call x1, Pallas kernels: 62.5 us -> 59.1 us  [local(): pl.pallas_call(functools.partial(kernel, dims), out_shape=jax.ShapeDtypeS...]
where the time goes in v2:
time: 67.3 us; the launch traced here: 66.1 us
  Pallas kernels  59.1 us (88%)
  local copies, waits for them, and re-layouts  4.96 us (7%)
  other arithmetic  2.07 us (3%)
    pallas_call x1, Pallas kernels, local(): pl.pallas_call(functools.partial(kernel, dims), out_shape=jax.ShapeDtypeS...  59.1 us
    unnamed x12, local copies, waits for them, and re-layouts  4.2 us

profile of v2, /device:TPU:0, one launch (start us, length us, event | category | flops | bytes accessed | tf_op | source)
XLA Modules:
  0.0 66.1 jit_solution(13570709002761801344)
XLA Ops:
  0.0 0.0 copy-start.3
  0.0 0.5 broadcast.63
  0.5 0.1 copy-done.3
  0.7 0.7 %reduce.3 = s32[16]{0:T(128)S(1)} reduce(s32[16,1]{0,1:T(1,128)S(1)} %copy-done.3, s32[]{:T(128)} %broadcast.63), dimensions={1}, to_apply=%param.11.reduce_sub_computation.3 | reduce | bytes 132 | tf_op args[3]
  1.3 0.0 copy-start.4
  1.3 0.6 copy-done.4
  2.0 0.1 pad.9.clone
  2.1 0.1 reshape_squeeze.3
  2.1 0.0 copy-start.2
  2.1 0.7 copy-done.2
  2.8 0.1 reshape.59
  2.9 0.1 pad_add_fusion
  3.0 0.0 copy-start
  3.0 0.1 copy.10
  3.0 0.6 copy-done
  3.7 0.1 rev.3
  3.8 0.1 broadcast_in_dim.24
  3.8 0.1 tile.20
  3.9 0.1 tile.22
  4.0 0.0 copy-start.1
  4.0 0.6 select_maximum_fusion.taps_ref
  4.6 0.1 copy-done.1
  4.7 0.1 tile.25
  4.8 0.7 %maximum_maximum_fusion.meta_ref = f32[16,128]{1,0:T(8,128)} fusion(f32[4,128]{1,0:T(4,128)S(1)} %tile.25, f32[4,128]{1,0:T(4,128)S(1)} %select_convert_fusion, f32[16]{0:T(128)S(1)} %pad.9.clone), kind=kLoop, calls=%fused_computation.1 | loop fusion | flops 4096 | bytes 12352 | tf_op jit(solution)/shard_map/concatenate | solution.py:333
  5.5 59.1 %shard_map.82 = f32[4,64,128]{2,1,0:T(8,128)} custom-call(f32[32,32,256]{2,1,0:T(8,128)} %bitcast.12, f32[16,128]{1,0:T(8,128)} %maximum_maximum_fusion.meta_ref, f32[12,2,256]{2,1,0:T(2,128)} %select_maximum_fusion.taps_ref, f32[3,4]{1,0:T(4,128)} %strength_ref.1, f32[128,128]{1,0:T(8,128)} %bitcast.13), custom_call_target="tpu_custom_call" | custom-call | tf_op jit(solution)/shard_map/pallas_call | solution.py:344
  64.6 1.6 %copy.12 = f32[4,64,128]{2,1,0:T(8,128)} copy(f32[4,64,128]{2,1,0:T(8,128)} %shard_map.82) | data formatting | bytes 262144
  (6 shorter events, 0.0 us)
Async XLA Ops:
  0.0 0.7 copy-start.3
  1.3 0.7 copy-start.4
  2.1 0.7 copy-start.2
  3.0 0.7 %copy-start = (f32[3,4,33]{2,1,0:T(4,128)S(1)}, f32[3,4,33]{2,1,0:T(4,128)}, u32[]{:S(2)}) copy-start(f32[3,4,33]{2,1,0:T(4,128)} %param.9) | copy-start | bytes 4756
  4.0 0.7 %copy-start.1 = (f32[1,4,4]{2,1,0:T(4,128)S(1)}, f32[1,4,4]{2,1,0:T(4,128)}, u32[]{:S(2)}) copy-start(f32[1,4,4]{2,1,0:T(4,128)} %param.14) | copy-start | bytes 196

commit v3 on v2

--- a/solution.py
+++ b/solution.py
@@ -43,8 +43,8 @@
 
 
 def kernel(
-    dims, x_ref, meta_ref, taps_ref, strength_ref, cols_ref, out_ref,
-    grid, row_h, row_l, col_h, col_l, meta_all, place_h, place_l, asm, stack, est, res,
+    dims, x_ref, dest_ref, off_ref, counts_ref, rows_ref, taps_ref, strength_ref, cols_ref, out_ref,
+    meta_ref, grid, row_h, row_l, col_h, col_l, meta_all, place_h, place_l, asm, stack, est, res,
     msend, mrecv, gsend, grecv, ssend, srecv, esend, erecv,
 ):
     S, D, C, T, B, RS, W, PASSES, radius, ppd, nch = dims
@@ -75,6 +75,29 @@
         return carry
 
     lax.fori_loop(1, n, greet, 0)
+
+    tile_rows = share * D * C
+    lane = lax.broadcasted_iota(jnp.int32, (1, rows), 1)
+    here = lax.div(lane, RS) == s
+    row_block = lax.div(lax.rem(lane, RS), BROWS)
+    count = off_ref.shape[0]
+    for half in range(2):
+        target = jnp.zeros((1, rows), jnp.int32)
+        first = jnp.zeros((1, rows), jnp.int32)
+        for j in range(half, count, 2):
+            hit = here & (row_block == j // 2)
+            target = jnp.where(hit, dest_ref[j, 0], target)
+            first = jnp.where(hit, dest_ref[j, 0] * tile_rows + off_ref[j], first)
+        meta_ref[half : half + 1, :] = target.astype(f32)
+        meta_ref[2 + half : 3 + half, :] = first.astype(f32)
+    for i in range(BROWS):
+        value = jnp.zeros((1, rows), f32)
+        for j in range(BROWS):
+            value = jnp.where(lax.rem(lane, BROWS) == j, rows_ref[0, i, j], value)
+        meta_ref[4 + i : 5 + i, :] = value
+    for t in range(T):
+        meta_ref[8 + t : 9 + t, :] = jnp.full((1, rows), counts_ref[t, 0], jnp.int32).astype(f32)
+
     pl.semaphore_wait(barrier, n - 1)
 
     md = s * D + d
@@ -140,7 +163,6 @@
 
     lax.fori_loop(1, S * D, meta_wait, 0)
 
-    tile_rows = share * D * C
     pieces = [meta_all[i * D + d, 0:8, :] for i in range(S)]
     total = pieces[0]
     for piece in pieces[1:]:
@@ -322,17 +344,6 @@
     nb = min(B, ppd)
     tile_rows = destinations.shape[0] * BROWS
     share = tile_rows // (D * C)
-    s = lax.axis_index("space")
-
-    target = destinations[:, 0].reshape(-1, 2).T
-    first = target * tile_rows + offsets.reshape(-1, 2).T
-    places = jnp.repeat(jnp.concatenate([target, first]), BROWS, axis=1)
-    strip = jnp.arange(rows)[None, :] // RS == s
-    places = jnp.where(strip, jnp.tile(places, (1, S)), 0).astype(f32)
-    tiled_rows = jnp.tile(resample_rows[0], (1, rows // BROWS))
-    meta = jnp.concatenate(
-        [places, tiled_rows, jnp.broadcast_to(counts.astype(f32), (T, rows))]
-    )
     width = max(W, rows)
     taps = jnp.stack([kernels, kernels[:, :, ::-1]], axis=2).reshape(PASSES * B, 2, tap_count)
     taps = jnp.pad(taps, ((0, 0), (0, 0), (0, width - tap_count)))
@@ -344,9 +355,10 @@
     return pl.pallas_call(
         functools.partial(kernel, dims),
         out_shape=jax.ShapeDtypeStruct((B, tile_rows, BCOLS), f32),
-        in_specs=[vmem, vmem, vmem, smem, vmem],
+        in_specs=[vmem, smem, smem, smem, smem, vmem, smem, vmem],
         out_specs=vmem,
         scratch_shapes=[
+            pltpu.VMEM((8 + T, rows), f32),
             pltpu.VMEM((ppd, rows, W), f32),
             pltpu.VMEM((PASSES * nb, rows, rows), bf16),
             pltpu.VMEM((PASSES * nb, rows, rows), bf16),
@@ -371,7 +383,7 @@
         compiler_params=pltpu.CompilerParams(
             collective_id=0, has_side_effects=True, vmem_limit_bytes=56 * 1024 * 1024
         ),
-    )(reflect.reshape(T * B, RS, W), meta, taps, strength, resample_columns[0])
+    )(reflect.reshape(T * B, RS, W), destinations, offsets, counts, resample_rows, taps, strength, resample_columns[0])
 
 
 def solution(mesh):

time: 67.3 us -> 65.1 us (0.967)
  other arithmetic: 2.07 us -> 0.63 us
    concatenate x2 -> x0, other arithmetic: 0.75 us -> none  [the longest x1 0.67 us: local(): jnp.concatenate([places, tiled_rows, jnp.broadcast_to(counts.astype(f32),...]
    unnamed x12 -> x7, local copies, waits for them, and re-layouts: 4.2 us -> 4.24 us
where the time goes in v3:
time: 65.1 us; the launch traced here: 64.1 us
  Pallas kernels  59.1 us (91%)
  local copies, waits for them, and re-layouts  4.33 us (7%)
    pallas_call x1, Pallas kernels, local(): pl.pallas_call(functools.partial(kernel, dims), out_shape=jax.ShapeDtypeS...  59.1 us
    unnamed x7, local copies, waits for them, and re-layouts  4.24 us

profile of v3, /device:TPU:0, one launch (start us, length us, event | category | flops | bytes accessed | tf_op | source)
XLA Modules:
  0.0 64.1 jit_solution(7737606961362183886)
XLA Ops:
  0.0 0.0 copy-start
  0.0 1.3 %copy.10.counts_ref = s32[8,1]{1,0:T(8,128)} copy(s32[8,1]{0,1:T(1,128)} %param.13) | data formatting | bytes 64 | tf_op args[5]
  1.3 0.0 copy-done
  1.3 0.1 rev.3
  1.4 0.0 copy-start.1
  1.4 0.7 %copy-done.1 = s32[16,1]{0,1:T(1,128)S(1)} copy-done((s32[16,1]{0,1:T(1,128)S(1)}, s32[16,1]{0,1:T(1,128)}, u32[]{:S(2)}) %copy-start.1) | copy-done | bytes 88
  2.1 0.7 %copy.9.dest_ref = s32[16,1]{1,0:T(8,128)} copy(s32[16,1]{0,1:T(1,128)S(1)} %copy-done.1) | data formatting | bytes 128 | tf_op args[3]
  2.8 0.6 select_maximum_fusion.taps_ref
  3.4 59.1 %shard_map.82 = f32[4,64,128]{2,1,0:T(8,128)} custom-call(f32[32,32,256]{2,1,0:T(8,128)} %bitcast.4, s32[16,1]{1,0:T(8,128)} %copy.9.dest_ref, s32[16]{0:T(128)} %off_ref.1, s32[8,1]{1,0:T(8,128)} %copy.10.counts_ref, f32[1,4,4]{2,1,0:T(4,128)} %rows_ref.1, f32[12,2,256]{2,1,0:T(2,128)} %select_maximum_fusion.taps_ref, f32[3,4]{1,0:T(4,128)} %strength_ref.1, ...), custom_call_target="tpu_custom_call" | custom-call | tf_op jit(solution)/shard_map/pallas_call | solution.py:355
  62.5 1.6 %copy.12 = f32[4,64,128]{2,1,0:T(8,128)} copy(f32[4,64,128]{2,1,0:T(8,128)} %shard_map.82) | data formatting | bytes 262144
Async XLA Ops:
  0.0 1.3 %copy-start = (f32[3,4,33]{2,1,0:T(4,128)S(1)}, f32[3,4,33]{2,1,0:T(4,128)}, u32[]{:S(2)}) copy-start(f32[3,4,33]{2,1,0:T(4,128)} %param.9) | copy-start | bytes 4756
  1.4 0.7 %copy-start.1 = (s32[16,1]{0,1:T(1,128)S(1)}, s32[16,1]{0,1:T(1,128)}, u32[]{:S(2)}) copy-start(s32[16,1]{0,1:T(1,128)} %param.11) | copy-start | bytes 196

commit v4 on v3

--- a/solution.py
+++ b/solution.py
@@ -86,8 +86,8 @@
         first = jnp.zeros((1, rows), jnp.int32)
         for j in range(half, count, 2):
             hit = here & (row_block == j // 2)
-            target = jnp.where(hit, dest_ref[j, 0], target)
-            first = jnp.where(hit, dest_ref[j, 0] * tile_rows + off_ref[j], first)
+            target = jnp.where(hit, dest_ref[j], target)
+            first = jnp.where(hit, dest_ref[j] * tile_rows + off_ref[j], first)
         meta_ref[half : half + 1, :] = target.astype(f32)
         meta_ref[2 + half : 3 + half, :] = first.astype(f32)
     for i in range(BROWS):
@@ -96,7 +96,7 @@
             value = jnp.where(lax.rem(lane, BROWS) == j, rows_ref[0, i, j], value)
         meta_ref[4 + i : 5 + i, :] = value
     for t in range(T):
-        meta_ref[8 + t : 9 + t, :] = jnp.full((1, rows), counts_ref[t, 0], jnp.int32).astype(f32)
+        meta_ref[8 + t : 9 + t, :] = jnp.full((1, rows), counts_ref[t], jnp.int32).astype(f32)
 
     pl.semaphore_wait(barrier, n - 1)
 
@@ -383,7 +383,7 @@
         compiler_params=pltpu.CompilerParams(
             collective_id=0, has_side_effects=True, vmem_limit_bytes=56 * 1024 * 1024
         ),
-    )(reflect.reshape(T * B, RS, W), destinations, offsets, counts, resample_rows, taps, strength, resample_columns[0])
+    )(reflect.reshape(T * B, RS, W), destinations[:, 0], offsets, counts[:, 0], resample_rows, taps, strength, resample_columns[0])
 
 
 def solution(mesh):

time: 65.1 us -> 63.1 us (0.969)
  local copies, waits for them, and re-layouts: 4.33 us -> 2.36 us
    unnamed x7 -> x3, local copies, waits for them, and re-layouts: 4.24 us -> 2.26 us
where the time goes in v4:
time: 63.1 us; the launch traced here: 62.1 us
  Pallas kernels  59.1 us (94%)
  local copies, waits for them, and re-layouts  2.36 us (4%)
    pallas_call x1, Pallas kernels, local(): pl.pallas_call(functools.partial(kernel, dims), out_shape=jax.ShapeDtypeS...  59.1 us
    unnamed x3, local copies, waits for them, and re-layouts  2.26 us

profile of v4, /device:TPU:0, one launch (start us, length us, event | category | flops | bytes accessed | tf_op | source)
XLA Modules:
  0.0 62.1 jit_solution(9285215606704937321)
XLA Ops:
  0.0 0.0 copy-start
  0.0 0.7 %copy-done = f32[3,4,33]{2,1,0:T(4,128)S(1)} copy-done((f32[3,4,33]{2,1,0:T(4,128)S(1)}, f32[3,4,33]{2,1,0:T(4,128)}, u32[]{:S(2)}) %copy-start) | copy-done | bytes 1608
  0.7 0.1 rev.3
  0.8 0.6 %select_maximum_fusion.taps_ref = f32[12,2,256]{2,1,0:T(2,128)} fusion(f32[12,1,33]{2,1,0:T(1,128)S(1)} %bitcast.9, f32[12,1,33]{2,1,0:T(1,128)S(1)} %bitcast.8), kind=kLoop, calls=%fused_computation | loop fusion | flops 24576 | bytes 27744 | tf_op jit(solution)/shard_map/stack | solution.py:348
  1.4 59.1 %shard_map.82 = f32[4,64,128]{2,1,0:T(8,128)} custom-call(f32[32,32,256]{2,1,0:T(8,128)} %bitcast.6, s32[16]{0:T(128)} %bitcast.10, s32[16]{0:T(128)} %off_ref.1, s32[8]{0:T(128)} %bitcast.11, f32[1,4,4]{2,1,0:T(4,128)} %rows_ref.1, f32[12,2,256]{2,1,0:T(2,128)} %select_maximum_fusion.taps_ref, f32[3,4]{1,0:T(4,128)} %strength_ref.1, f32[128,128]{1,0:T(8,128)} %bitcast.7), custom_call_target="tpu_custom_call" | custom-call | tf_op jit(solution)/shard_map/pallas_call | solution.py:355
  60.5 1.6 %copy.10 = f32[4,64,128]{2,1,0:T(8,128)} copy(f32[4,64,128]{2,1,0:T(8,128)} %shard_map.82) | data formatting | bytes 262144
Async XLA Ops:
  0.0 0.7 %copy-start = (f32[3,4,33]{2,1,0:T(4,128)S(1)}, f32[3,4,33]{2,1,0:T(4,128)}, u32[]{:S(2)}) copy-start(f32[3,4,33]{2,1,0:T(4,128)} %param.9) | copy-start | bytes 4756
